TPU v7x, 32 devices: a whole 2x2x4 slice. The times are simulated.
32 devices in a mesh: segment: 2 (over x), expert: 8 (over z, y), dp: 2 (over core).
Axes of the slice: x: 2, y: 2, z: 4, core: 2. Of those that a mesh axis runs over, the one named last changes fastest.
Arguments:
- entering: bfloat16 [2, 1024, 2560], P('segment', ('expert', 'dp')), may hold values from -0.59765625 to 0.59765625
- fresh: bfloat16 [1, 1024, 2560], P(None, ('expert', 'dp')), may hold values from -0.59765625 to 0.59765625
- w_gate: bfloat16 [2, 16, 2560, 768], P('segment', ('expert', 'dp')), may hold values from -0.125 to 0.125
- w_up: bfloat16 [2, 16, 2560, 768], P('segment', ('expert', 'dp')), may hold values from -0.125 to 0.125
- w_down: bfloat16 [2, 16, 768, 2560], P('segment', ('expert', 'dp')), may hold values from -0.21875 to 0.21875
- router: bfloat16 [2, 2560, 16], P('segment'), may hold values from -0.0625 to 0.0625
- gain: float32 [2, 2560], P('segment'), may hold values from 0.5 to 2
- routes: int32 [2, 2, 1024, 6], P('segment', None, ('expert', 'dp')), may hold values from 0 to 15, all different within a row; in each aligned block of 64 rows (0 to 63, 64 to 127, ..., all dimensions but the last counted through in order) at most 32 rows name the same one
Outputs:
- section_out: bfloat16 [2, 2, 1024, 2560], P('segment', None, ('expert', 'dp'))
Inputs may be any that keep to these rules, and one draw needn't show every extreme that they name: `routes`: in every aligned block of 64 rows (the tokens of one device for one section and micro-batch) no expert is named by more than 32 rows, and in some blocks one expert is named by exactly 32 rows; a row names 6 different experts.
All inputs are finite; a program needn't handle non-finite values.
Results may differ from a plain program's by a relative error of at most 0.009.
Values may be sent and summed in bfloat16 or wider, within the bound.
A program may use at most 64 MiB of HBM per device.

v0:
```python
import jax
import jax.numpy as jnp
from jax import lax
from jax.sharding import PartitionSpec as P


def shifted(value, axis, steps):
    count = lax.axis_size(axis)
    leading, last = (max(0, -steps), min(count, count - steps))
    return lax.ppermute(value, axis, [(source, source + steps) for source in range(leading, last)])


def expert_rows(slot_rows, gate_weight, up_weight, down_weight):
    model_width = slot_rows.shape[-1]
    flattened = slot_rows.reshape(-1, model_width)
    gate_out = jnp.dot(flattened, gate_weight, preferred_element_type=jnp.float32)
    upper = jnp.dot(flattened, up_weight, preferred_element_type=jnp.float32)
    hidden = (jax.nn.silu(gate_out) * upper).astype(jnp.bfloat16)
    projected = jnp.dot(hidden, down_weight, preferred_element_type=jnp.float32).astype(
        jnp.bfloat16
    )
    return projected.reshape(slot_rows.shape)


def routed_slots(chosen_ids, expert_count):
    onehot = (chosen_ids[:, None] == jnp.arange(expert_count, dtype=jnp.int32)[None, :]).astype(
        jnp.int32
    )
    before = jnp.cumsum(onehot, axis=0) - onehot
    return jnp.sum(before * onehot, axis=1)


def section(incoming, gate_weight, up_weight, down_weight, router_layer, gain_layer, chosen_ids):
    tok_rows, model_width = incoming.shape
    top_count = chosen_ids.shape[1]
    experts = router_layer.shape[1]
    capacity = 4 * tok_rows * top_count // (3 * experts)
    values = incoming.astype(jnp.float32)
    inv_scale = lax.rsqrt(jnp.mean(values * values, axis=1, keepdims=True) + 1e-06)
    normed = (values * inv_scale * gain_layer[None, :]).astype(jnp.bfloat16)
    logits = jnp.dot(normed, router_layer, preferred_element_type=jnp.float32)
    scores = jax.nn.sigmoid(logits)
    chosen = jnp.take_along_axis(scores, chosen_ids, axis=1)
    mixing = chosen / jnp.sum(chosen, axis=1, keepdims=True)
    flat_picks = chosen_ids.reshape(-1)
    slot_ids = routed_slots(flat_picks, experts)
    owners = jnp.arange(tok_rows * top_count, dtype=jnp.int32) // top_count
    source = jnp.full((experts, capacity), tok_rows, jnp.int32).at[flat_picks, slot_ids].set(owners)
    padded = jnp.concatenate([normed, jnp.zeros((1, model_width), jnp.bfloat16)], axis=0)
    outgoing = padded[source]
    processed = expert_rows(
        lax.all_to_all(outgoing, ("expert", "dp"), split_axis=0, concat_axis=0, tiled=True),
        gate_weight,
        up_weight,
        down_weight,
    )
    returned = lax.all_to_all(processed, ("expert", "dp"), split_axis=0, concat_axis=0, tiled=True)
    landed = returned[flat_picks, slot_ids].reshape(tok_rows, top_count, model_width)
    summed = values + jnp.sum(landed.astype(jnp.float32) * mixing[:, :, None], axis=1)
    return summed.astype(jnp.bfloat16)


def shards(entering, fresh, w_gate, w_up, w_down, router, gain, routes):
    segment_id = lax.axis_index("segment")
    micro_count = routes.shape[1]
    current = entering[0]
    results = []
    for step_index in range(micro_count):
        if step_index > 0:
            arrived = shifted(results[-1], "segment", 1)
            current = jnp.where(segment_id == 0, fresh[step_index - 1], arrived)
        output = section(
            current,
            w_gate[0, 0],
            w_up[0, 0],
            w_down[0, 0],
            router[0],
            gain[0],
            routes[0, step_index],
        )
        results.append(output)
    return jnp.stack(results)[None]


def solution(mesh):
    in_specs = (
        P("segment", ("expert", "dp"), None),
        P(None, ("expert", "dp"), None),
        P("segment", ("expert", "dp"), None, None),
        P("segment", ("expert", "dp"), None, None),
        P("segment", ("expert", "dp"), None, None),
        P("segment", None, None),
        P("segment", None),
        P("segment", None, ("expert", "dp"), None),
    )
    out_specs = P("segment", None, ("expert", "dp"), None)
    return jax.shard_map(shards, mesh=mesh, in_specs=in_specs, out_specs=out_specs, check_vma=False)
```

profile of v0, /device:TPU:10, one launch (start us, length us, event | category | flops | bytes accessed | tf_op | source)
XLA Modules:
  0.0 371.9 jit_solution(10996757420032658949)
XLA Ops:
  1.8 1.1 fusion.23
  3.0 0.9 reduce-window.16
  4.2 0.9 reduce-window.14
  5.5 20.0 %scatter_fusion = s32[16,32]{1,0:T(8,128)S(1)} fusion(s32[16,32]{1,0:T(8,128)S(1)} %broadcast.157.clone, s32[384]{0:T(512)S(1)} %get-tuple-element.14, s32[384]{0:T(512)S(1)} %add_select_fusion), kind=kCustom, calls=%fused_computation.6 | custom fusion | bytes 7680 | tf_op jit(solution)/shard_map/scatter | solution.py:48
  25.9 2.6 gather_fusion
  28.5 64.9 %all_to_all.20 = bf16[16,32,2560]{2,1,0:T(8,128)(2,1)S(1)} all-to-all(bf16[16,32,2560]{2,1,0:T(8,128)(2,1)S(1)} %bitcast.153), channel_id=1, replica_groups=mesh['segment'=2,'expert'=8,'dp'=2] {'expert','dp'}, dimensions={0} | all-to-all | bytes 5242880 | tf_op jit(solution)/shard_map/all_to_all | solution.py:52
  93.5 1.5 copy-done.7
  95.0 2.2 fusion.8
  97.2 11.2 %convolution_convert_fusion.1 = bf16[512,2560]{1,0:T(8,128)(2,1)} fusion(bf16[1,1,768,2560]{3,2,1,0:T(8,128)(2,1)} %param.14, f32[512,768]{1,0:T(8,128)S(1)} %fusion.8, bf16[512,2560]{1,0:T(8,128)(2,1)} %bitcast.158, bf16[1,1,2560,768]{3,2,1,0:T(8,128)(2,1)} %param.13), kind=kOutput, calls=%fused_computation.11 | convolution fusion | flops 4030201856 | bytes 14680064 | tf_op jit(solution)/shard_map/dot_general | solution.py:19
  108.4 5.1 %all-to-all-start.1 = ((bf16[16,32,2560]{2,1,0:T(8,128)(2,1)}), bf16[16,32,2560]{2,1,0:T(8,128)(2,1)S(1)}, u32[]{:S(2)}, u32[]{:S(2)}) async-start(bf16[16,32,2560]{2,1,0:T(8,128)(2,1)} %bitcast.155), calls=%async_computation.1 | async-start | bytes 5242880 | tf_op jit(solution)/shard_map/all_to_all | solution.py:57
  114.0 3.0 gather_fusion.4
  117.4 20.0 %scatter_fusion.1 = s32[16,32]{1,0:T(8,128)S(1)} fusion(s32[16,32]{1,0:T(8,128)S(1)} %broadcast.157.clone.1, s32[384]{0:T(512)S(1)} %get-tuple-element.7, s32[384]{0:T(512)S(1)} %add_select_fusion), kind=kCustom, calls=%fused_computation.7 | custom fusion | bytes 7680 | tf_op jit(solution)/shard_map/scatter | solution.py:48
  137.4 33.2 %all-to-all-done.1 = bf16[16,32,2560]{2,1,0:T(8,128)(2,1)S(1)} async-done(((bf16[16,32,2560]{2,1,0:T(8,128)(2,1)}), bf16[16,32,2560]{2,1,0:T(8,128)(2,1)S(1)}, u32[]{:S(2)}, u32[]{:S(2)}) %all-to-all-start.1) | async-done | bytes 2621472 | tf_op jit(solution)/shard_map/all_to_all | solution.py:57
  170.6 11.5 %gather_fusion.1 = bf16[384,2560]{1,0:T(8,128)(2,1)} fusion(bf16[16,32,2560]{2,1,0:T(8,128)(2,1)S(1)} %all-to-all-done.1, s32[384]{0:T(512)S(1)} %get-tuple-element.15), kind=kCustom, calls=%fused_computation.3 | custom fusion | bytes 3935232 | tf_op jit(solution)/shard_map/gather | solution.py:58
  182.1 4.5 %reshape.187 = f32[64,6,2560]{2,1,0:T(8,128)} reshape(bf16[384,2560]{1,0:T(8,128)(2,1)} %gather_fusion.1) | data formatting | bytes 5898240 | tf_op jit(solution)/shard_map/convert_element_type | solution.py:59
  186.6 4.4 %multiply_reduce_fusion.1 = f32[64,2560]{1,0:T(8,128)S(1)} fusion(f32[64,6,2560]{2,1,0:T(8,128)} %reshape.187, f32[64,6]{1,0:T(8,128)S(1)} %copy.18), kind=kLoop, calls=%fused_computation.9 | loop fusion | flops 1802240 | bytes 4589056 | tf_op jit(solution)/shard_map/reduce_sum | solution.py:59
  192.0 1.3 collective-permute-start
  193.4 9.7 %collective-permute-done = bf16[64,2560]{1,0:T(8,128)(2,1)S(1)} collective-permute-done((bf16[64,2560]{1,0:T(8,128)(2,1)S(1)}, bf16[64,2560]{1,0:T(8,128)(2,1)S(1)}, u32[]{:S(2)}, u32[]{:S(2)}) %collective-permute-start) | collective-permute-done | bytes 327712 | tf_op jit(solution)/shard_map/ppermute | solution.py:10
  204.8 2.6 gather_fusion.2
  207.5 65.8 %all_to_all.21 = bf16[16,32,2560]{2,1,0:T(8,128)(2,1)S(1)} all-to-all(bf16[16,32,2560]{2,1,0:T(8,128)(2,1)S(1)} %bitcast.154), channel_id=1, replica_groups=mesh['segment'=2,'expert'=8,'dp'=2] {'expert','dp'}, dimensions={0} | all-to-all | bytes 5242880 | tf_op jit(solution)/shard_map/all_to_all | solution.py:52
  273.2 1.5 copy-done.8
  274.8 2.2 fusion.6
  277.0 11.2 %convolution_convert_fusion = bf16[512,2560]{1,0:T(8,128)(2,1)} fusion(bf16[1,1,768,2560]{3,2,1,0:T(8,128)(2,1)} %param.14, f32[512,768]{1,0:T(8,128)S(1)} %fusion.6, bf16[512,2560]{1,0:T(8,128)(2,1)} %bitcast.160, bf16[1,1,2560,768]{3,2,1,0:T(8,128)(2,1)} %param.13), kind=kOutput, calls=%fused_computation.10 | convolution fusion | flops 4030201856 | bytes 14680064 | tf_op jit(solution)/shard_map/dot_general | solution.py:19
  288.1 5.2 %all-to-all-start.3 = ((bf16[16,32,2560]{2,1,0:T(8,128)(2,1)}), bf16[16,32,2560]{2,1,0:T(8,128)(2,1)S(1)}, u32[]{:S(2)}, u32[]{:S(2)}) async-start(bf16[16,32,2560]{2,1,0:T(8,128)(2,1)} %bitcast.156), calls=%async_computation.3 | async-start | bytes 5242880 | tf_op jit(solution)/shard_map/all_to_all | solution.py:57
  293.6 1.8 fusion.29
  295.4 1.1 fusion.16
  296.5 3.0 gather_fusion.5
  299.9 50.6 %all-to-all-done.3 = bf16[16,32,2560]{2,1,0:T(8,128)(2,1)S(1)} async-done(((bf16[16,32,2560]{2,1,0:T(8,128)(2,1)}), bf16[16,32,2560]{2,1,0:T(8,128)(2,1)S(1)}, u32[]{:S(2)}, u32[]{:S(2)}) %all-to-all-start.3) | async-done | bytes 2621472 | tf_op jit(solution)/shard_map/all_to_all | solution.py:57
  350.5 11.5 %gather_fusion.3 = bf16[384,2560]{1,0:T(8,128)(2,1)} fusion(bf16[16,32,2560]{2,1,0:T(8,128)(2,1)S(1)} %all-to-all-done.3, s32[384]{0:T(512)S(1)} %get-tuple-element.6), kind=kCustom, calls=%fused_computation.5 | custom fusion | bytes 3935232 | tf_op jit(solution)/shard_map/gather | solution.py:58
  362.0 4.5 %reshape.188 = f32[64,6,2560]{2,1,0:T(8,128)} reshape(bf16[384,2560]{1,0:T(8,128)(2,1)} %gather_fusion.3) | data formatting | bytes 5898240 | tf_op jit(solution)/shard_map/convert_element_type | solution.py:59
  366.5 4.5 %multiply_reduce_fusion = f32[64,2560]{1,0:T(8,128)S(1)} fusion(f32[64,6,2560]{2,1,0:T(8,128)} %reshape.188, f32[64,6]{1,0:T(8,128)S(1)} %copy.26), kind=kLoop, calls=%fused_computation.8 | loop fusion | flops 1802240 | bytes 4589056 | tf_op jit(solution)/shard_map/reduce_sum | solution.py:59
  371.0 0.9 maximum_bitcast_fusion
  (79 shorter events, 7.1 us)
Async XLA Ops:
  0.0 113.7 %copy-start = (bf16[1,2560,16]{1,2,0:T(8,128)(2,1)S(1)}, bf16[1,2560,16]{1,2,0:T(8,128)(2,1)}, u32[]{:S(2)}) copy-start(bf16[1,2560,16]{1,2,0:T(8,128)(2,1)} %param.15) | copy-start | bytes 245764
  1.2 24.5 %copy-start.11 = (f32[1,2560]{1,0:T(1,128)S(1)}, f32[1,2560]{1,0:T(1,128)}, u32[]{:S(2)}) copy-start(f32[1,2560]{1,0:T(1,128)} %param.16) | copy-start | bytes 30724
  1.3 24.4 %copy-start.3 = (bf16[1,64,2560]{2,1,0:T(8,128)(2,1)S(1)}, bf16[1,64,2560]{2,1,0:T(8,128)(2,1)}, u32[]{:S(2)}) copy-start(bf16[1,64,2560]{2,1,0:T(8,128)(2,1)} %param.10) | copy-start | bytes 983044
  28.5 66.5 %copy-start.12 = (bf16[1,1,2560,768]{3,2,1,0:T(8,128)(2,1)S(1)}, bf16[1,1,2560,768]{3,2,1,0:T(8,128)(2,1)}, u32[]{:S(2)}) copy-start(bf16[1,1,2560,768]{3,2,1,0:T(8,128)(2,1)} %param.12) | copy-start | bytes 11796484
  93.5 1.5 copy-start.7
  108.4 62.2 %all-to-all-start.1 = ((bf16[16,32,2560]{2,1,0:T(8,128)(2,1)}), bf16[16,32,2560]{2,1,0:T(8,128)(2,1)S(1)}, u32[]{:S(2)}, u32[]{:S(2)}) async-start(bf16[16,32,2560]{2,1,0:T(8,128)(2,1)} %bitcast.155), calls=%async_computation.1 | async-start | bytes 5242880 | tf_op jit(solution)/shard_map/all_to_all | solution.py:57
  186.6 16.5 %copy-start.10 = (bf16[1,64,2560]{2,1,0:T(8,128)(2,1)S(1)}, bf16[1,64,2560]{2,1,0:T(8,128)(2,1)}, u32[]{:S(2)}) copy-start(bf16[1,64,2560]{2,1,0:T(8,128)(2,1)} %param.11) | copy-start | bytes 983044
  191.0 0.8 copy-start.1
  192.0 11.1 %collective-permute-start = (bf16[64,2560]{1,0:T(8,128)(2,1)S(1)}, bf16[64,2560]{1,0:T(8,128)(2,1)S(1)}, u32[]{:S(2)}, u32[]{:S(2)}) collective-permute-start(bf16[64,2560]{1,0:T(8,128)(2,1)S(1)} %fusion.26), channel_id=1, source_target_pairs={{0,16},{1,17},{2,18},{3,19},{4,20},{5,21},{6,22},{7,23},{8,24},{9,... | collective-permute-start | bytes 983048 | tf_op jit(solution)/shard_map/ppermute | solution.py:10
  203.3 0.7 copy-start.4
  204.1 0.7 copy-start.6
  207.5 67.3 %copy-start.13 = (bf16[1,1,2560,768]{3,2,1,0:T(8,128)(2,1)S(1)}, bf16[1,1,2560,768]{3,2,1,0:T(8,128)(2,1)}, u32[]{:S(2)}) copy-start(bf16[1,1,2560,768]{3,2,1,0:T(8,128)(2,1)} %param.12) | copy-start | bytes 11796484
  273.2 1.5 copy-start.8
  288.1 5.5 %copy-start.2 = (f32[64,2560]{1,0:T(8,128)S(1)}, f32[64,2560]{1,0:T(8,128)}, u32[]{:S(2)}) copy-start(f32[64,2560]{1,0:T(8,128)} %copy-done.1) | copy-start | bytes 1966084
  288.1 62.4 %all-to-all-start.3 = ((bf16[16,32,2560]{2,1,0:T(8,128)(2,1)}), bf16[16,32,2560]{2,1,0:T(8,128)(2,1)S(1)}, u32[]{:S(2)}, u32[]{:S(2)}) async-start(bf16[16,32,2560]{2,1,0:T(8,128)(2,1)} %bitcast.156), calls=%async_computation.3 | async-start | bytes 5242880 | tf_op jit(solution)/shard_map/all_to_all | solution.py:57
  366.5 4.5 %copy-start.5 = (bf16[64,2560]{1,0:T(8,128)(2,1)S(1)}, bf16[64,2560]{1,0:T(8,128)(2,1)}, u32[]{:S(2)}) copy-start(bf16[64,2560]{1,0:T(8,128)(2,1)} %copy-done.4) | copy-start | bytes 983044
  366.5 4.5 %copy-start.9 = (bf16[1,64,2560]{2,1,0:T(8,128)(2,1)S(1)}, bf16[1,64,2560]{2,1,0:T(8,128)(2,1)}, u32[]{:S(2)}) copy-start(bf16[1,64,2560]{2,1,0:T(8,128)(2,1)} %fusion.29) | copy-start | bytes 983044
where the time goes:
time: 374 us; the launch traced here: 372 us
  blocking collectives  131 us (35%)
  waiting for transfers between devices  93.5 us (25%)
  local copies, waits for them, and re-layouts  92 us (25%)
  matrix products  28.2 us (8%)
  other arithmetic  15.6 us (4%)
  starting transfers between devices  11.6 us (3%)
    all_to_all x2, blocking collectives, section(): lax.all_to_all(outgoing, ('expert', 'dp'), split_axis=0, concat_axis=0, t...  131 us
    all_to_all x2, waiting for transfers between devices, section(): lax.all_to_all(processed, ('expert', 'dp'), split_axis=0, concat_axis=0,...  83.8 us
    scatter x2, local copies, waits for them, and re-layouts, section(): jnp.full((experts, capacity), tok_rows, jnp.int32).at[flat_picks, slot_ids]  40 us
    gather x2, local copies, waits for them, and re-layouts, section(): returned[flat_picks, slot_ids].reshape(tok_rows, top_count, model_width)  23 us
    dot_general x2, matrix products, expert_rows(): jnp.dot(hidden, down_weight, preferred_element_type=jnp.float32)  22.4 us
    all_to_all x2, starting transfers between devices, section(): lax.all_to_all(processed, ('expert', 'dp'), split_axis=0, concat_axis=0,...  10.4 us
    ppermute x1, waiting for transfers between devices, shifted(): lax.ppermute(value, axis, [(source, source + steps) for source in range(l...  9.75 us
    convert_element_type x2, local copies, waits for them, and re-layouts, section(): landed.astype(jnp.float32) * mixing[:, :, None]  8.97 us
  transfers between devices with their start and end apart: 3, of which 3 were waited for; matrix products, arithmetic and copies ran while one was open for 8% of the time, Pallas kernels for 0%

commit v1 on v0

--- a/solution.py
+++ b/solution.py
@@ -60,8 +60,39 @@
     return summed.astype(jnp.bfloat16)
 
 
+def mixed_weights(normed, router_layer, chosen_ids):
+    experts = router_layer.shape[1]
+    logits = jnp.dot(normed, router_layer, preferred_element_type=jnp.float32)
+    ids = jnp.arange(experts, dtype=jnp.int32)
+    named = jnp.any(chosen_ids[:, :, None] == ids[None, None, :], axis=1)
+    scores = jnp.where(named, jax.nn.sigmoid(logits), 0.0)
+    return scores / jnp.sum(scores, axis=1, keepdims=True)
+
+
+def gathered_section(
+    incoming, gate_weight, up_weight, down_weight, router_layer, gain_layer, chosen_ids
+):
+    values = incoming.astype(jnp.float32)
+    inv_scale = lax.rsqrt(jnp.mean(values * values, axis=1, keepdims=True) + 1e-06)
+    normed = (values * inv_scale * gain_layer[None, :]).astype(jnp.bfloat16)
+    mixing = mixed_weights(normed, router_layer, chosen_ids)
+    axes = ("expert", "dp")
+    tokens = lax.all_gather(normed, axes, axis=0, tiled=True)
+    mine = lax.all_to_all(mixing.T, axes, split_axis=0, concat_axis=1, tiled=True)
+    gate_out = jnp.dot(tokens, gate_weight, preferred_element_type=jnp.float32)
+    upper = jnp.dot(tokens, up_weight, preferred_element_type=jnp.float32)
+    hidden = (jax.nn.silu(gate_out) * upper).astype(jnp.bfloat16)
+    projected = jnp.dot(hidden, down_weight, preferred_element_type=jnp.float32)
+    shares = (projected * mine.reshape(-1, 1)).astype(jnp.bfloat16)
+    summed = lax.psum_scatter(shares, axes, scatter_dimension=0, tiled=True)
+    return (values + summed.astype(jnp.float32)).astype(jnp.bfloat16)
+
+
 def shards(entering, fresh, w_gate, w_up, w_down, router, gain, routes):
     segment_id = lax.axis_index("segment")
+    tok_rows, top_count = routes.shape[2:]
+    capacity = 4 * tok_rows * top_count // (3 * router.shape[2])
+    layer = gathered_section if tok_rows <= 2 * capacity else section
     micro_count = routes.shape[1]
     current = entering[0]
     results = []
@@ -69,7 +100,7 @@
         if step_index > 0:
             arrived = shifted(results[-1], "segment", 1)
             current = jnp.where(segment_id == 0, fresh[step_index - 1], arrived)
-        output = section(
+        output = layer(
             current,
             w_gate[0, 0],
             w_up[0, 0],

time: 374 us -> 337 us (0.901)
  waiting for transfers between devices: 93.5 us -> 249 us
  blocking collectives: 131 us -> 21.1 us
  local copies, waits for them, and re-layouts: 92 us -> 1.55 us
  between operations: 0.35 us -> 13.3 us
  matrix products: 28.2 us -> 38.4 us
  starting transfers between devices: 11.6 us -> 1.42 us
  other arithmetic: 15.6 us -> 9.33 us
    reduce_scatter x0 -> x2, waiting for transfers between devices: none -> 153 us  [gathered_section(): summed = lax.psum_scatter(shares, axes, scatter_dimension=0, tiled=True)]
    all_to_all x2, blocking collectives: 131 us -> 21.1 us  [gathered_section(): lax.all_to_all(mixing.T, axes, split_axis=0, concat_axis=1, tiled=True)]
    all_gather x0 -> x2, waiting for transfers between devices: none -> 87 us  [gathered_section(): tokens = lax.all_gather(normed, axes, axis=0, tiled=True)]
    all_to_all x2 -> x0, waiting for transfers between devices: 83.8 us -> none  [section(): lax.all_to_all(processed, ('expert', 'dp'), split_axis=0, concat_axis=0,...]
    scatter x2 -> x0, local copies, waits for them, and re-layouts: 40 us -> none  [section(): jnp.full((experts, capacity), tok_rows, jnp.int32).at[flat_picks, slot_ids]]
    gather x14 -> x0, local copies, waits for them, and re-layouts: 35.1 us -> none  [the longest x2 23 us: section(): returned[flat_picks, slot_ids].reshape(tok_rows, top_count, model_width)]
    all_to_all x2 -> x0, starting transfers between devices: 10.4 us -> none  [section(): lax.all_to_all(processed, ('expert', 'dp'), split_axis=0, concat_axis=0,...]
    dot_general x6 -> x8, matrix products: 28.2 us -> 38.4 us  [the longest x2 14.9 us: gathered_section(): upper = jnp.dot(tokens, up_weight, preferred_element_type=jnp.float32)]
  transfers between devices with their start and end apart: 3 -> 5, of which waited for: 3 -> 5; matrix products, arithmetic and copies ran while one was open for 8% -> 2% of each run, Pallas kernels for 0% -> 0%
where the time goes in v1:
time: 337 us; the launch traced here: 334 us
  waiting for transfers between devices  249 us (74%)
  matrix products  38.4 us (11%)
  blocking collectives  21.1 us (6%)
  between operations  13.3 us (4%)
  other arithmetic  9.33 us (3%)
    reduce_scatter x2, waiting for transfers between devices, gathered_section(): summed = lax.psum_scatter(shares, axes, scatter_dimension=0, tiled=True)  153 us
    all_gather x2, waiting for transfers between devices, gathered_section(): tokens = lax.all_gather(normed, axes, axis=0, tiled=True)  87 us
    all_to_all x2, blocking collectives, gathered_section(): lax.all_to_all(mixing.T, axes, split_axis=0, concat_axis=1, tiled=True)  21.1 us
    dot_general x2, matrix products, gathered_section(): upper = jnp.dot(tokens, up_weight, preferred_element_type=jnp.float32)  14.9 us
    dot_general x2, matrix products, gathered_section(): projected = jnp.dot(hidden, down_weight, preferred_element_type=jnp.float32)  12 us
    ppermute x1, waiting for transfers between devices, shifted(): lax.ppermute(value, axis, [(source, source + steps) for source in range(l...  9.12 us
    dot_general x2, matrix products, gathered_section(): gate_out = jnp.dot(tokens, gate_weight, preferred_element_type=jnp.float32)  9.05 us
  transfers between devices with their start and end apart: 5, of which 5 were waited for; matrix products, arithmetic and copies ran while one was open for 2% of the time, Pallas kernels for 0%

profile of v1, /device:TPU:10, one launch (start us, length us, event | category | flops | bytes accessed | tf_op | source)
XLA Modules:
  0.0 334.3 jit_solution(12183325363913064763)
XLA Ops:
  6.5 1.2 fusion.25
  7.7 0.7 reduce
  8.5 1.8 fusion.27
  10.3 0.0 reduce-scatter.3.cloned.1.call-start
  10.4 0.8 fusion.44
  11.2 1.3 fusion.45
  12.5 11.1 %all_to_all.26 = f32[16,1,64]{2,1,0:T(1,128)S(1)} all-to-all(f32[16,1,64]{2,1,0:T(1,128)S(1)} %bitcast.81), channel_id=1, replica_groups=mesh['segment'=2,'expert'=8,'dp'=2] {'expert','dp'}, dimensions={0} | all-to-all | bytes 8192 | tf_op jit(solution)/shard_map/all_to_all | solution.py:81
  23.6 0.6 broadcast.80
  24.2 0.7 reduce.7
  24.9 0.1 mul.93
  24.9 42.8 %all-gather.3.cloned.1.call-done = bf16[1024,2560]{1,0:T(8,128)(2,1)} async-done(((bf16[64,2560]{1,0:T(8,128)(2,1)}), bf16[1024,2560]{1,0:T(8,128)(2,1)}) %all-gather.3.cloned.1.call-update) | async-done | bytes 5242896 | tf_op jit(solution)/shard_map/all_gather | solution.py:80
  67.8 7.5 %fusion.4 = f32[1024,768]{1,0:T(8,128)S(1)} fusion(bf16[1024,2560]{1,0:T(8,128)(2,1)} %all-gather.3.cloned.1.call-done, bf16[1,1,2560,768]{3,2,1,0:T(8,128)(2,1)} %param.11), kind=kOutput, calls=%fused_computation.6 | convolution fusion | flops 4026531840 | bytes 12320768 | tf_op jit(solution)/shard_map/dot_general | solution.py:83
  75.3 4.5 %multiply_convert_fusion.3 = bf16[1024,768]{1,0:T(8,128)(2,1)S(1)} fusion(f32[1024,768]{1,0:T(8,128)S(1)} %fusion.4, bf16[1024,2560]{1,0:T(8,128)(2,1)S(1)} %copy-done.3, bf16[1,1,2560,768]{3,2,1,0:T(8,128)(2,1)S(1)} %copy-done.5), kind=kOutput, calls=%fused_computation.13 | convolution fusion | flops 4031250432 | bytes 13893632 | tf_op jit(solution)/shard_map/dot_general | solution.py:82
  79.8 6.0 %multiply_convert_fusion.1 = bf16[1024,2560]{1,0:T(8,128)(2,1)} fusion(bf16[1024,768]{1,0:T(8,128)(2,1)S(1)} %multiply_convert_fusion.3, f32[1024]{0:T(1024)S(1)} %mul.93, bf16[1,1,768,2560]{3,2,1,0:T(8,128)(2,1)S(1)} %copy-done.7), kind=kOutput, calls=%fused_computation.1 | convolution fusion | flops 4031774720 | bytes 10752000 | tf_op jit(solution)/shard_map/dot_general | solution.py:85
  85.9 76.4 %reduce-scatter.3.cloned.1.call-done = bf16[64,2560]{1,0:T(8,128)(2,1)} async-done(((bf16[1024,2560]{1,0:T(8,128)(2,1)}), bf16[64,2560]{1,0:T(8,128)(2,1)}) %reduce-scatter.3.cloned.1.call-update) | async-done | bytes 327696 | tf_op jit(solution)/shard_map/reduce_scatter | solution.py:87
  162.3 1.0 fusion.28
  163.4 1.3 collective-permute-start
  164.7 9.1 %collective-permute-done = bf16[64,2560]{1,0:T(8,128)(2,1)S(1)} collective-permute-done((bf16[64,2560]{1,0:T(8,128)(2,1)S(1)}, bf16[64,2560]{1,0:T(8,128)(2,1)S(1)}, u32[]{:S(2)}, u32[]{:S(2)}) %collective-permute-start) | collective-permute-done | bytes 327712 | tf_op jit(solution)/shard_map/ppermute | solution.py:10
  173.8 0.2 fusion.31
  174.1 0.9 fusion.33
  175.0 0.0 reduce-scatter.5.cloned.1.call-start
  175.0 1.2 fusion.46
  176.2 10.0 %all_to_all.27 = f32[16,1,64]{2,1,0:T(1,128)S(1)} all-to-all(f32[16,1,64]{2,1,0:T(1,128)S(1)} %bitcast.82), channel_id=1, replica_groups=mesh['segment'=2,'expert'=8,'dp'=2] {'expert','dp'}, dimensions={0} | all-to-all | bytes 8192 | tf_op jit(solution)/shard_map/all_to_all | solution.py:81
  186.2 0.7 reduce.8
  187.0 0.1 mul.102
  187.0 44.2 %all-gather.5.cloned.1.call-done = bf16[1024,2560]{1,0:T(8,128)(2,1)} async-done(((bf16[64,2560]{1,0:T(8,128)(2,1)}), bf16[1024,2560]{1,0:T(8,128)(2,1)}) %all-gather.5.cloned.1.call-update) | async-done | bytes 5242896 | tf_op jit(solution)/shard_map/all_gather | solution.py:80
  231.2 7.5 %fusion.2 = f32[1024,768]{1,0:T(8,128)S(1)} fusion(bf16[1024,2560]{1,0:T(8,128)(2,1)} %all-gather.5.cloned.1.call-done, bf16[1,1,2560,768]{3,2,1,0:T(8,128)(2,1)} %param.11), kind=kOutput, calls=%fused_computation.4 | convolution fusion | flops 4026531840 | bytes 12320768 | tf_op jit(solution)/shard_map/dot_general | solution.py:83
  238.7 4.5 %multiply_convert_fusion.2 = bf16[1024,768]{1,0:T(8,128)(2,1)S(1)} fusion(f32[1024,768]{1,0:T(8,128)S(1)} %fusion.2, bf16[1024,2560]{1,0:T(8,128)(2,1)S(1)} %copy-done.4, bf16[1,1,2560,768]{3,2,1,0:T(8,128)(2,1)S(1)} %copy-done.6), kind=kOutput, calls=%fused_computation.12 | convolution fusion | flops 4031250432 | bytes 13893632 | tf_op jit(solution)/shard_map/dot_general | solution.py:82
  243.2 6.0 %multiply_convert_fusion = bf16[1024,2560]{1,0:T(8,128)(2,1)} fusion(bf16[1024,768]{1,0:T(8,128)(2,1)S(1)} %multiply_convert_fusion.2, f32[1024]{0:T(1024)S(1)} %mul.102, bf16[1,1,768,2560]{3,2,1,0:T(8,128)(2,1)S(1)} %copy-done.8), kind=kOutput, calls=%fused_computation | convolution fusion | flops 4031774720 | bytes 10752000 | tf_op jit(solution)/shard_map/dot_general | solution.py:85
  249.3 76.5 %reduce-scatter.5.cloned.1.call-done = bf16[64,2560]{1,0:T(8,128)(2,1)} async-done(((bf16[1024,2560]{1,0:T(8,128)(2,1)}), bf16[64,2560]{1,0:T(8,128)(2,1)}) %reduce-scatter.5.cloned.1.call-update) | async-done | bytes 327696 | tf_op jit(solution)/shard_map/reduce_scatter | solution.py:87
  325.8 1.0 fusion.35
  326.9 0.9 maximum_bitcast_fusion
  (32 shorter events, 0.2 us)
Async XLA Ops:
  6.5 4.7 %copy-start = (bf16[1,2560,16]{1,2,0:T(8,128)(2,1)S(1)}, bf16[1,2560,16]{1,2,0:T(8,128)(2,1)}, u32[]{:S(2)}) copy-start(bf16[1,2560,16]{1,2,0:T(8,128)(2,1)} %param.13) | copy-start | bytes 245764
  6.5 61.2 %all-gather.3.cloned.1.call-start = ((), (), s32[]{:S(2)}) async-start(), calls=%async_computation.4 | async-start | bytes 5570560 | tf_op jit(solution)/shard_map/all_gather | solution.py:80
  10.3 152.0 %reduce-scatter.3.cloned.1.call-start = ((), (), s32[]{:S(2)}) async-start(), calls=%async_computation.5 | async-start | bytes 5570560 | tf_op jit(solution)/shard_map/reduce_scatter | solution.py:87
  67.8 7.5 %copy-start.3 = (bf16[1024,2560]{1,0:T(8,128)(2,1)S(1)}, bf16[1024,2560]{1,0:T(8,128)(2,1)}, u32[]{:S(2)}) copy-start(bf16[1024,2560]{1,0:T(8,128)(2,1)} %all-gather.3.cloned.1.call-done) | copy-start | bytes 15728644
  67.8 7.5 %copy-start.5 = (bf16[1,1,2560,768]{3,2,1,0:T(8,128)(2,1)S(1)}, bf16[1,1,2560,768]{3,2,1,0:T(8,128)(2,1)}, u32[]{:S(2)}) copy-start(bf16[1,1,2560,768]{3,2,1,0:T(8,128)(2,1)} %param.10) | copy-start | bytes 11796484
  75.3 4.5 %copy-start.7 = (bf16[1,1,768,2560]{3,2,1,0:T(8,128)(2,1)S(1)}, bf16[1,1,768,2560]{3,2,1,0:T(8,128)(2,1)}, u32[]{:S(2)}) copy-start(bf16[1,1,768,2560]{3,2,1,0:T(8,128)(2,1)} %param.12) | copy-start | bytes 11796484
  85.8 76.5 %copy-start.1 = (bf16[1,64,2560]{2,1,0:T(8,128)(2,1)S(1)}, bf16[1,64,2560]{2,1,0:T(8,128)(2,1)}, u32[]{:S(2)}) copy-start(bf16[1,64,2560]{2,1,0:T(8,128)(2,1)} %param.8) | copy-start | bytes 983044
  85.8 88.0 %copy-start.2 = (bf16[1,64,2560]{2,1,0:T(8,128)(2,1)S(1)}, bf16[1,64,2560]{2,1,0:T(8,128)(2,1)}, u32[]{:S(2)}) copy-start(bf16[1,64,2560]{2,1,0:T(8,128)(2,1)} %param.9) | copy-start | bytes 983044
  85.8 145.3 %all-gather.5.cloned.1.call-start = ((), (), s32[]{:S(2)}) async-start(), calls=%async_computation.6 | async-start | bytes 5570560 | tf_op jit(solution)/shard_map/all_gather | solution.py:80
  163.4 10.4 %collective-permute-start = (bf16[64,2560]{1,0:T(8,128)(2,1)S(1)}, bf16[64,2560]{1,0:T(8,128)(2,1)S(1)}, u32[]{:S(2)}, u32[]{:S(2)}) collective-permute-start(bf16[64,2560]{1,0:T(8,128)(2,1)S(1)} %fusion.28), channel_id=1, source_target_pairs={{0,16},{1,17},{2,18},{3,19},{4,20},{5,21},{6,22},{7,23},{8,24},{9,... | collective-permute-start | bytes 983048 | tf_op jit(solution)/shard_map/ppermute | solution.py:10
  175.0 150.9 %reduce-scatter.5.cloned.1.call-start = ((), (), s32[]{:S(2)}) async-start(), calls=%async_computation.7 | async-start | bytes 5570560 | tf_op jit(solution)/shard_map/reduce_scatter | solution.py:87
  231.2 7.5 %copy-start.4 = (bf16[1024,2560]{1,0:T(8,128)(2,1)S(1)}, bf16[1024,2560]{1,0:T(8,128)(2,1)}, u32[]{:S(2)}) copy-start(bf16[1024,2560]{1,0:T(8,128)(2,1)} %all-gather.5.cloned.1.call-done) | copy-start | bytes 15728644
  231.2 7.5 %copy-start.6 = (bf16[1,1,2560,768]{3,2,1,0:T(8,128)(2,1)S(1)}, bf16[1,1,2560,768]{3,2,1,0:T(8,128)(2,1)}, u32[]{:S(2)}) copy-start(bf16[1,1,2560,768]{3,2,1,0:T(8,128)(2,1)} %param.10) | copy-start | bytes 11796484
  238.7 4.5 %copy-start.8 = (bf16[1,1,768,2560]{3,2,1,0:T(8,128)(2,1)S(1)}, bf16[1,1,768,2560]{3,2,1,0:T(8,128)(2,1)}, u32[]{:S(2)}) copy-start(bf16[1,1,768,2560]{3,2,1,0:T(8,128)(2,1)} %param.12) | copy-start | bytes 11796484
Sparse Core Ops, SparseCore 0:
  10.5 57.2 all-gather.2
  86.0 76.3 reduce-scatter.2
  175.1 56.0 all-gather.4
  249.4 76.3 reduce-scatter.4

commit v2 on v0

--- a/solution.py
+++ b/solution.py
@@ -1,6 +1,10 @@
+import functools
+
 import jax
 import jax.numpy as jnp
 from jax import lax
+from jax.experimental import pallas as pl
+from jax.experimental.pallas import tpu as pltpu
 from jax.sharding import PartitionSpec as P
 
 
@@ -82,6 +86,395 @@
     return jnp.stack(results)[None]
 
 
+LANES = 128
+MESH = pl.DeviceIdType.MESH
+
+
+def near_first(order, z, nz):
+    low, high = z, nz - 1 - z
+    paired = 2 * jnp.minimum(low, high)
+    step = (order + 1) // 2
+    beside = z + step * (2 * (order % 2) - 1)
+    beyond = jnp.where(high > low, order, nz - 1 - order)
+    return jnp.where(order <= paired, beside, beyond)
+
+
+def fused_kernel(
+    nz,
+    segments,
+    experts,
+    entering_ref,
+    fresh_ref,
+    mask_ref,
+    router_ref,
+    gain_ref,
+    gate_hbm,
+    up_hbm,
+    down_hbm,
+    out_ref,
+    tokens,
+    parts,
+    core_in,
+    y_in,
+    z_in,
+    x_in,
+    hidden,
+    gate_w,
+    up_w,
+    down_w,
+    w_sem,
+    za_s,
+    za_r,
+    ya_s,
+    ya_r,
+    ca_s,
+    ca_r,
+    cp_s,
+    cp_r,
+    yp_s,
+    yp_r,
+    zp_s,
+    zp_r,
+    x_s,
+    x_r,
+):
+    micro, rows, width = out_ref.shape
+    hid = gate_w.shape[1]
+    seg, e, c = lax.axis_index("segment"), lax.axis_index("expert"), lax.axis_index("dp")
+    z, y = e // 2, e % 2
+    expert_id = 2 * e + c
+    tile = 256
+
+    def at(start, size):
+        return pl.ds(pl.multiple_of(start, rows), size)
+
+    half = c * 2 * rows
+    own = at(half + y * rows, rows)
+    other = at(half + (1 - y) * rows, rows)
+    sibling = (seg, e, 1 - c)
+    across = (seg, 2 * z + 1 - y, c)
+
+    def line(direction):
+        return (seg, e + 2 * (1 - 2 * direction), c)
+
+    def remote(src, dst, send, recv, target):
+        return pltpu.make_async_remote_copy(
+            src_ref=src,
+            dst_ref=dst,
+            send_sem=send,
+            recv_sem=recv,
+            device_id=target,
+            device_id_type=MESH,
+        )
+
+    def z_tokens(p, t, k):
+        block = tokens.at[p, t, own]
+        return remote(block, block, za_s.at[p, k, t], za_r.at[p, k, t], line(k))
+
+    def y_tokens(p, t):
+        block = tokens.at[p, t, own]
+        return remote(block, block, ya_s.at[p, t], ya_r.at[p, t], across)
+
+    def c_tokens(p, t, yy):
+        block = tokens.at[p, t, at(half + yy * rows, rows)]
+        return remote(block, block, ca_s.at[p, t, yy], ca_r.at[p, t, yy], sibling)
+
+    def c_parts(p, t):
+        src = parts.at[p, t, at((1 - c) * 2 * rows, 2 * rows)]
+        return remote(src, core_in.at[p, t], cp_s.at[p, t], cp_r.at[p, t], sibling)
+
+    def y_parts(p, t):
+        return remote(parts.at[p, t, other], y_in.at[p, t], yp_s.at[p, t], yp_r.at[p, t], across)
+
+    def z_parts(p, t, k):
+        return remote(
+            parts.at[p, t, own], z_in.at[p, k, t], zp_s.at[p, k, t], zp_r.at[p, k, t], line(k)
+        )
+
+    def x_out(p):
+        return remote(out_ref.at[p], x_in.at[p], x_s.at[p], x_r.at[p], (seg + 1, e, c))
+
+    loads = [
+        pltpu.make_async_copy(src.at[0, 0], dst, w_sem.at[n])
+        for n, (src, dst) in enumerate(((gate_hbm, gate_w), (up_hbm, up_w), (down_hbm, down_w)))
+    ]
+    for load in loads:
+        load.start()
+
+    barrier = pltpu.get_barrier_semaphore()
+
+    def greet(target):
+        pl.semaphore_signal(barrier, inc=1, device_id=target, device_id_type=MESH)
+
+    greet(sibling)
+    greet(across)
+    for present, target in (
+        (z < nz - 1, line(0)),
+        (z > 0, line(1)),
+        (seg < segments - 1, (seg + 1, e, c)),
+        (seg > 0, (seg - 1, e, c)),
+    ):
+        pl.when(present)(functools.partial(greet, target))
+    peers = 2
+    for places in (z, nz - 1 - z, seg, segments - 1 - seg):
+        peers = peers + jnp.minimum(places, 1)
+    pl.semaphore_wait(barrier, peers)
+
+    lanes = lax.broadcasted_iota(jnp.int32, (rows, LANES), 1)
+    plane_lanes = lax.broadcasted_iota(jnp.int32, (4 * rows, LANES), 1)
+
+    def normalise(p, source):
+        values = source[...].astype(jnp.float32)
+        inv_scale = lax.rsqrt(jnp.mean(values * values, axis=1, keepdims=True) + 1e-06)
+        normed = (values * inv_scale * gain_ref[...]).astype(jnp.bfloat16)
+        tokens[p, z, own, :width] = normed
+        logits = jnp.dot(normed, router_ref[...], preferred_element_type=jnp.float32)
+        scores = jnp.where(mask_ref[p] > 0.0, 1.0 / (1.0 + jnp.exp(-logits)), 0.0)
+        total = jnp.sum(jnp.where(lanes < experts, scores, 0.0), axis=1, keepdims=True)
+        mixing = scores / total
+        rounded = mixing.astype(jnp.bfloat16).astype(jnp.float32)
+        coded = jnp.where(lanes < experts, rounded, mixing - rounded)
+        tokens[p, z, own, width:] = coded.astype(jnp.bfloat16)
+
+    def acquire(p, t):
+        @pl.when(t < z)
+        def _():
+            z_tokens(p, t, 0).wait_recv()
+
+        @pl.when(t > z)
+        def _():
+            z_tokens(p, t, 1).wait_recv()
+
+        @pl.when((t <= z) & (z < nz - 1))
+        def _():
+            z_tokens(p, t, 0).start()
+
+        @pl.when((t >= z) & (z > 0))
+        def _():
+            z_tokens(p, t, 1).start()
+
+        y_tokens(p, t).start()
+        c_tokens(p, t, y).start()
+
+    def finish(p, t, between):
+        y_tokens(p, t).wait_recv()
+        c_tokens(p, t, 1 - y).start()
+        between()
+        c_tokens(p, t, 0).wait_recv()
+        c_tokens(p, t, 1).wait_recv()
+        coded = tokens[p, t, :, width:].astype(jnp.float32)
+        mine = (plane_lanes == expert_id) | (plane_lanes == expert_id + experts)
+        weight = jnp.sum(jnp.where(mine, coded, 0.0), axis=1, keepdims=True)
+
+        @pl.loop(0, hid // tile)
+        def _(n):
+            columns = pl.ds(pl.multiple_of(n * tile, tile), tile)
+            block = tokens[p, t, :, :width]
+            gate = jnp.dot(block, gate_w[:, columns], preferred_element_type=jnp.float32)
+            upper = jnp.dot(block, up_w[:, columns], preferred_element_type=jnp.float32)
+            hidden[:, columns] = (gate / (1.0 + jnp.exp(-gate)) * upper).astype(jnp.bfloat16)
+
+        @pl.loop(0, width // tile)
+        def _(n):
+            columns = pl.ds(pl.multiple_of(n * tile, tile), tile)
+            projected = jnp.dot(
+                hidden[...], down_w[:, columns], preferred_element_type=jnp.float32
+            )
+            parts[p, t, :, columns] = (projected * weight).astype(jnp.bfloat16)
+
+        c_parts(p, t).start()
+
+    def both_cores(p, t):
+        c_parts(p, t).wait_recv()
+
+        @pl.loop(0, 2 * rows // 16)
+        def _(n):
+            here = pl.ds(pl.multiple_of(half + n * 16, 16), 16)
+            there = pl.ds(pl.multiple_of(n * 16, 16), 16)
+            parts[p, t, here] = (
+                parts[p, t, here].astype(jnp.float32) + core_in[p, t, there].astype(jnp.float32)
+            ).astype(jnp.bfloat16)
+
+        y_parts(p, t).start()
+
+    def along_line(p, t):
+        y_parts(p, t).wait_recv()
+
+        def total(received):
+            @pl.loop(0, rows // 16)
+            def _(n):
+                here = pl.ds(pl.multiple_of(half + y * rows + n * 16, 16), 16)
+                there = pl.ds(pl.multiple_of(n * 16, 16), 16)
+                value = parts[p, t, here].astype(jnp.float32)
+                value = value + y_in[p, t, there].astype(jnp.float32)
+                if received is not None:
+                    value = value + z_in[p, received, t, there].astype(jnp.float32)
+                parts[p, t, here] = value.astype(jnp.bfloat16)
+
+        for k, beyond, outermost in ((0, t > z, z == 0), (1, t < z, z == nz - 1)):
+
+            @pl.when(beyond & outermost)
+            def _(k=k):
+                total(None)
+                z_parts(p, t, k).start()
+
+            @pl.when(beyond & jnp.logical_not(outermost))
+            def _(k=k):
+                z_parts(p, t, k).wait_recv()
+                total(k)
+                z_parts(p, t, k).start()
+
+    def complete(p, source):
+        y_parts(p, z).wait_recv()
+        pl.when(z > 0)(lambda: z_parts(p, z, 0).wait_recv())
+        pl.when(z < nz - 1)(lambda: z_parts(p, z, 1).wait_recv())
+
+        def add(received):
+            @pl.loop(0, rows // 16)
+            def _(n):
+                here = pl.ds(pl.multiple_of(half + y * rows + n * 16, 16), 16)
+                there = pl.ds(pl.multiple_of(n * 16, 16), 16)
+                value = source[there].astype(jnp.float32)
+                value = value + parts[p, z, here].astype(jnp.float32)
+                value = value + y_in[p, z, there].astype(jnp.float32)
+                for k in received:
+                    value = value + z_in[p, k, z, there].astype(jnp.float32)
+                out_ref[p, there] = value.astype(jnp.bfloat16)
+
+        pl.when(z == 0)(lambda: add((1,)))
+        pl.when(z == nz - 1)(lambda: add((0,)))
+        pl.when((z > 0) & (z < nz - 1))(lambda: add((0, 1)))
+
+    for p in range(micro):
+        source = x_in.at[p]
+        if p == 0:
+            source = entering_ref
+        else:
+
+            @pl.when(seg == 0)
+            def _(p=p):
+                x_in[p] = fresh_ref[p - 1]
+
+            @pl.when(seg > 0)
+            def _(p=p):
+                x_out(p - 1).wait_recv()
+                x_in[p] = x_in[p - 1]
+
+        normalise(p, source)
+        acquire(p, z)
+
+        @pl.loop(1, nz)
+        def _(order, p=p):
+            acquire(p, near_first(order, z, nz))
+            if p == 0:
+
+                @pl.when(order == 1)
+                def _():
+                    for load in loads:
+                        load.wait()
+
+            finish(p, near_first(order - 1, z, nz), lambda: None)
+
+        finish(p, near_first(nz - 1, z, nz), lambda: both_cores(p, z))
+
+        @pl.loop(1, nz)
+        def _(back, p=p):
+            both_cores(p, near_first(nz - back, z, nz))
+
+        @pl.loop(1, nz)
+        def _(back, p=p):
+            along_line(p, near_first(nz - back, z, nz))
+
+        complete(p, source)
+        if p < micro - 1:
+
+            @pl.when(seg < segments - 1)
+            def _(p=p):
+                x_out(p).start()
+
+    for p in range(micro):
+
+        @pl.loop(0, nz)
+        def _(t, p=p):
+            @pl.when((t <= z) & (z < nz - 1))
+            def _():
+                z_tokens(p, t, 0).wait_send()
+
+            @pl.when((t >= z) & (z > 0))
+            def _():
+                z_tokens(p, t, 1).wait_send()
+
+            y_tokens(p, t).wait_send()
+            c_tokens(p, t, 0).wait_send()
+            c_tokens(p, t, 1).wait_send()
+            c_parts(p, t).wait_send()
+            y_parts(p, t).wait_send()
+
+            @pl.when(t > z)
+            def _():
+                z_parts(p, t, 0).wait_send()
+
+            @pl.when(t < z)
+            def _():
+                z_parts(p, t, 1).wait_send()
+
+        if p < micro - 1:
+
+            @pl.when(seg < segments - 1)
+            def _(p=p):
+                x_out(p).wait_send()
+
+
+def fused_shards(nz, entering, fresh, w_gate, w_up, w_down, router, gain, routes):
+    micro, rows, top_count = routes.shape[1:]
+    width, experts = router.shape[1:]
+    hid = w_gate.shape[3]
+    segments = lax.axis_size("segment")
+    ids = jnp.arange(LANES, dtype=jnp.int32)
+    ids = jnp.where(ids < 2 * experts, ids % experts, -1)
+    mask = jnp.any(routes[0][:, :, :, None] == ids[None, None, None, :], axis=2)
+    spare = jnp.zeros((width, LANES - 2 * experts), jnp.bfloat16)
+    doubled = jnp.concatenate([router[0], router[0], spare], axis=1)
+    bf16 = jnp.bfloat16
+    vmem = pl.BlockSpec(memory_space=pltpu.VMEM)
+    hbm = pl.BlockSpec(memory_space=pl.ANY)
+    sem = pltpu.SemaphoreType.DMA
+    out = pl.pallas_call(
+        functools.partial(fused_kernel, nz, segments, experts),
+        out_shape=jax.ShapeDtypeStruct((micro, rows, width), bf16),
+        in_specs=[vmem] * 5 + [hbm] * 3,
+        out_specs=vmem,
+        scratch_shapes=[
+            pltpu.VMEM((micro, nz, 4 * rows, width + LANES), bf16),
+            pltpu.VMEM((micro, nz, 4 * rows, width), bf16),
+            pltpu.VMEM((micro, nz, 2 * rows, width), bf16),
+            pltpu.VMEM((micro, nz, rows, width), bf16),
+            pltpu.VMEM((micro, 2, nz, rows, width), bf16),
+            pltpu.VMEM((micro, rows, width), bf16),
+            pltpu.VMEM((4 * rows, hid), bf16),
+            pltpu.VMEM((width, hid), bf16),
+            pltpu.VMEM((width, hid), bf16),
+            pltpu.VMEM((hid, width), bf16),
+            sem((3,)),
+        ]
+        + [sem((micro, 2, nz))] * 2
+        + [sem((micro, nz))] * 2
+        + [sem((micro, nz, 2))] * 2
+        + [sem((micro, nz))] * 4
+        + [sem((micro, 2, nz))] * 2
+        + [sem((micro,))] * 2,
+        compiler_params=pltpu.CompilerParams(
+            collective_id=0, has_side_effects=True, vmem_limit_bytes=60 * 1024 * 1024
+        ),
+        cost_estimate=pl.CostEstimate(
+            flops=6 * micro * nz * 4 * rows * width * hid,
+            bytes_accessed=6 * width * hid,
+            transcendentals=micro * nz * 4 * rows * hid,
+        ),
+    )(entering[0], fresh, mask.astype(jnp.float32), doubled, gain, w_gate, w_up, w_down)
+    return out[None]
+
+
 def solution(mesh):
     in_specs = (
         P("segment", ("expert", "dp"), None),
@@ -94,4 +487,9 @@
         P("segment", None, ("expert", "dp"), None),
     )
     out_specs = P("segment", None, ("expert", "dp"), None)
-    return jax.shard_map(shards, mesh=mesh, in_specs=in_specs, out_specs=out_specs, check_vma=False)
+    positions = {getattr(device, "coords", (0, 0, 0))[1] for device in mesh.devices.flat}
+    line = mesh.shape["expert"] // 2
+    body = shards
+    if len(positions) == 2 and mesh.shape["dp"] == 2 and 2 <= line <= 4:
+        body = functools.partial(fused_shards, line)
+    return jax.shard_map(body, mesh=mesh, in_specs=in_specs, out_specs=out_specs, check_vma=False)

time: 374 us -> 188 us (0.50)
  Pallas kernels: 0 us -> 180 us
  blocking collectives: 131 us -> 0 us
  waiting for transfers between devices: 93.5 us -> 0 us
  local copies, waits for them, and re-layouts: 92 us -> 3.27 us
  matrix products: 28.2 us -> 0 us
  other arithmetic: 15.6 us -> 2.04 us
  starting transfers between devices: 11.6 us -> 0 us
    pallas_call x0 -> x1, Pallas kernels: none -> 180 us  [fused_shards(): pl.pallas_call(functools.partial(fused_kernel, nz, segments, experts), ou...]
    all_to_all x2 -> x0, blocking collectives: 131 us -> none  [section(): lax.all_to_all(outgoing, ('expert', 'dp'), split_axis=0, concat_axis=0, t...]
    all_to_all x2 -> x0, waiting for transfers between devices: 83.8 us -> none  [section(): lax.all_to_all(processed, ('expert', 'dp'), split_axis=0, concat_axis=0,...]
    scatter x2 -> x0, local copies, waits for them, and re-layouts: 40 us -> none  [section(): jnp.full((experts, capacity), tok_rows, jnp.int32).at[flat_picks, slot_ids]]
    gather x14 -> x0, local copies, waits for them, and re-layouts: 35.1 us -> none  [the longest x2 23 us: section(): returned[flat_picks, slot_ids].reshape(tok_rows, top_count, model_width)]
    dot_general x6 -> x0, matrix products: 28.2 us -> none  [the longest x2 22.4 us: expert_rows(): jnp.dot(hidden, down_weight, preferred_element_type=jnp.float32)]
    reduce_sum x8 -> x0, other arithmetic: 10.5 us -> none  [the longest x2 8.9 us: section(): jnp.sum(landed.astype(jnp.float32) * mixing[:, :, None], axis=1)]
    all_to_all x2 -> x0, starting transfers between devices: 10.4 us -> none  [section(): lax.all_to_all(processed, ('expert', 'dp'), split_axis=0, concat_axis=0,...]
  transfers between devices with their start and end apart: 3 -> 0, of which waited for: 3 -> 0; matrix products, arithmetic and copies ran while one was open for 8% -> 0% of each run, Pallas kernels for 0% -> 0%
where the time goes in v2:
time: 188 us; the launch traced here: 186 us
  Pallas kernels  180 us (96%)
  local copies, waits for them, and re-layouts  3.27 us (2%)
  other arithmetic  2.04 us (1%)
    pallas_call x1, Pallas kernels, fused_shards(): pl.pallas_call(functools.partial(fused_kernel, nz, segments, experts), ou...  180 us

profile of v2, /device:TPU:10, one launch (start us, length us, event | category | flops | bytes accessed | tf_op | source)
XLA Modules:
  0.0 185.5 jit_solution(10149202187161778440)
XLA Ops:
  0.0 0.0 copy-start
  0.0 1.2 copy.12
  1.2 0.1 pad.2.clone
  1.3 1.2 maximum_maximum_fusion.router_ref
  2.6 0.0 copy-done
  2.6 0.2 compare_reduce_fusion
  2.7 0.6 convert_element_type.3.mask_ref
  3.4 180.2 %shard_map.82 = bf16[2,64,2560]{2,1,0:T(8,128)(2,1)} custom-call(bf16[64,2560]{1,0:T(8,128)(2,1)} %bitcast.7, bf16[1,64,2560]{2,1,0:T(8,128)(2,1)} %fresh_ref.1, f32[2,64,128]{2,1,0:T(8,128)} %convert_element_type.3.mask_ref, bf16[2560,128]{1,0:T(8,128)(2,1)} %maximum_maximum_fusion.router_ref, f32[1,2560]{1,0:T(1,128)} %gain_ref.1, ...), custom_call_target="tpu_custom_call" | custom-call | flops 24159191040 | bytes 11796480 | tf_op jit(solution)/shard_map/pallas_call | solution.py:442
  183.6 2.0 %copy.14 = bf16[1,2,64,2560]{3,2,1,0:T(8,128)(2,1)} copy(bf16[1,2,64,2560]{3,2,1,0:T(8,128)(2,1)} %bitcast.5) | data formatting | bytes 1310720
  (3 shorter events, 0.0 us)
Async XLA Ops:
  0.0 2.6 %copy-start = (s32[1,2,64,6]{2,1,3,0:T(2,128)S(1)}, s32[1,2,64,6]{2,1,3,0:T(2,128)}, u32[]{:S(2)}) copy-start(s32[1,2,64,6]{2,1,3,0:T(2,128)} %param.15) | copy-start | bytes 9220

commit v3 on v2

--- a/solution.py
+++ b/solution.py
@@ -105,7 +105,7 @@
     experts,
     entering_ref,
     fresh_ref,
-    mask_ref,
+    routes_ref,
     router_ref,
     gain_ref,
     gate_hbm,
@@ -119,6 +119,7 @@
     z_in,
     x_in,
     hidden,
+    router_w,
     gate_w,
     up_w,
     down_w,
@@ -194,6 +195,9 @@
     def x_out(p):
         return remote(out_ref.at[p], x_in.at[p], x_s.at[p], x_r.at[p], (seg + 1, e, c))
 
+    router_w[...] = jnp.zeros_like(router_w)
+    router_w[:experts] = router_ref[...]
+    router_w[experts : 2 * experts] = router_ref[...]
     loads = [
         pltpu.make_async_copy(src.at[0, 0], dst, w_sem.at[n])
         for n, (src, dst) in enumerate(((gate_hbm, gate_w), (up_hbm, up_w), (down_hbm, down_w)))
@@ -228,8 +232,18 @@
         inv_scale = lax.rsqrt(jnp.mean(values * values, axis=1, keepdims=True) + 1e-06)
         normed = (values * inv_scale * gain_ref[...]).astype(jnp.bfloat16)
         tokens[p, z, own, :width] = normed
-        logits = jnp.dot(normed, router_ref[...], preferred_element_type=jnp.float32)
-        scores = jnp.where(mask_ref[p] > 0.0, 1.0 / (1.0 + jnp.exp(-logits)), 0.0)
+        logits = lax.dot_general(
+            normed,
+            router_w[...],
+            (((1,), (1,)), ((), ())),
+            preferred_element_type=jnp.float32,
+        )
+        chosen = routes_ref[p]
+        ids = jnp.where(lanes < experts, lanes, lanes - experts)
+        named = chosen[:, :1] == ids
+        for n in range(1, chosen.shape[1]):
+            named = named | (chosen[:, n : n + 1] == ids)
+        scores = jnp.where(named, 1.0 / (1.0 + jnp.exp(-logits)), 0.0)
         total = jnp.sum(jnp.where(lanes < experts, scores, 0.0), axis=1, keepdims=True)
         mixing = scores / total
         rounded = mixing.astype(jnp.bfloat16).astype(jnp.float32)
@@ -295,11 +309,7 @@
                 parts[p, t, here].astype(jnp.float32) + core_in[p, t, there].astype(jnp.float32)
             ).astype(jnp.bfloat16)
 
-        y_parts(p, t).start()
-
     def along_line(p, t):
-        y_parts(p, t).wait_recv()
-
         def total(received):
             @pl.loop(0, rows // 16)
             def _(n):
@@ -364,26 +374,36 @@
         acquire(p, z)
 
         @pl.loop(1, nz)
-        def _(order, p=p):
-            acquire(p, near_first(order, z, nz))
+        def _(distance, p=p):
+            pl.when(z + distance < nz)(lambda: acquire(p, z + distance))
+            pl.when(z >= distance)(lambda: acquire(p, z - distance))
             if p == 0:
 
-                @pl.when(order == 1)
+                @pl.when(distance == 1)
                 def _():
                     for load in loads:
                         load.wait()
 
-            finish(p, near_first(order - 1, z, nz), lambda: None)
-
-        finish(p, near_first(nz - 1, z, nz), lambda: both_cores(p, z))
+            finish(p, near_first(distance - 1, z, nz), lambda: None)
+
+        def own_plane(p=p):
+            both_cores(p, z)
+            y_parts(p, z).start()
+
+        farthest = near_first(nz - 1, z, nz)
+        finish(p, farthest, own_plane)
+        both_cores(p, farthest)
+        y_parts(p, farthest).start()
 
         @pl.loop(1, nz)
         def _(back, p=p):
-            both_cores(p, near_first(nz - back, z, nz))
-
-        @pl.loop(1, nz)
-        def _(back, p=p):
-            along_line(p, near_first(nz - back, z, nz))
+            t = near_first(nz - back, z, nz)
+            following = near_first(nz - back - 1, z, nz)
+            more = back < nz - 1
+            pl.when(more)(lambda: both_cores(p, following))
+            y_parts(p, t).wait_recv()
+            pl.when(more)(lambda: y_parts(p, following).start())
+            along_line(p, t)
 
         complete(p, source)
         if p < micro - 1:
@@ -430,11 +450,6 @@
     width, experts = router.shape[1:]
     hid = w_gate.shape[3]
     segments = lax.axis_size("segment")
-    ids = jnp.arange(LANES, dtype=jnp.int32)
-    ids = jnp.where(ids < 2 * experts, ids % experts, -1)
-    mask = jnp.any(routes[0][:, :, :, None] == ids[None, None, None, :], axis=2)
-    spare = jnp.zeros((width, LANES - 2 * experts), jnp.bfloat16)
-    doubled = jnp.concatenate([router[0], router[0], spare], axis=1)
     bf16 = jnp.bfloat16
     vmem = pl.BlockSpec(memory_space=pltpu.VMEM)
     hbm = pl.BlockSpec(memory_space=pl.ANY)
@@ -452,6 +467,7 @@
             pltpu.VMEM((micro, 2, nz, rows, width), bf16),
             pltpu.VMEM((micro, rows, width), bf16),
             pltpu.VMEM((4 * rows, hid), bf16),
+            pltpu.VMEM((LANES, width), bf16),
             pltpu.VMEM((width, hid), bf16),
             pltpu.VMEM((width, hid), bf16),
             pltpu.VMEM((hid, width), bf16),
@@ -471,7 +487,7 @@
             bytes_accessed=6 * width * hid,
             transcendentals=micro * nz * 4 * rows * hid,
         ),
-    )(entering[0], fresh, mask.astype(jnp.float32), doubled, gain, w_gate, w_up, w_down)
+    )(entering[0], fresh, routes[0], router[0].T, gain, w_gate, w_up, w_down)
     return out[None]
 
 

time: 188 us -> 171 us (0.910); the launches traced: 186 us -> 171 us
  Pallas kernels: 180 us -> 167 us
  other arithmetic: 2.04 us -> 0 us
    pallas_call x1, Pallas kernels: 180 us -> 167 us  [fused_shards(): pl.pallas_call(functools.partial(fused_kernel, nz, segments, experts), ou...]
where the time goes in v3:
time: 171 us
  Pallas kernels  167 us (98%)
  local copies, waits for them, and re-layouts  3.39 us (2%)
    pallas_call x1, Pallas kernels, fused_shards(): pl.pallas_call(functools.partial(fused_kernel, nz, segments, experts), ou...  167 us

profile of v3, /device:TPU:10, one launch (start us, length us, event | category | flops | bytes accessed | tf_op | source)
XLA Modules:
  0.0 170.8 jit_solution(4824003458782732033)
XLA Ops:
  0.0 1.4 copy.9
  1.4 167.4 %shard_map.82 = bf16[2,64,2560]{2,1,0:T(8,128)(2,1)} custom-call(bf16[64,2560]{1,0:T(8,128)(2,1)} %bitcast.8, bf16[1,64,2560]{2,1,0:T(8,128)(2,1)} %fresh_ref.1, s32[2,64,6]{2,1,0:T(8,128)} %bitcast.7, bf16[16,2560]{1,0:T(8,128)(2,1)} %bitcast.9, f32[1,2560]{1,0:T(1,128)} %gain_ref.1, bf16[1,1,2560,768]{3,2,1,0:T(8,128)(2,1)} %gate_hbm.1, ...), custom_call_target="tpu_custom_call" | custom-call | flops 24159191040 | bytes 11796480 | tf_op jit(solution)/shard_map/pallas_call | solution.py:457
  168.8 2.0 %copy.11 = bf16[1,2,64,2560]{3,2,1,0:T(8,128)(2,1)} copy(bf16[1,2,64,2560]{3,2,1,0:T(8,128)(2,1)} %bitcast.6) | data formatting | bytes 1310720

commit v4 on v3

--- a/solution.py
+++ b/solution.py
@@ -187,9 +187,16 @@
     def y_parts(p, t):
         return remote(parts.at[p, t, other], y_in.at[p, t], yp_s.at[p, t], yp_r.at[p, t], across)
 
-    def z_parts(p, t, k):
+    piece = rows // 2
+
+    def z_parts(p, t, k, h):
+        start = pl.multiple_of(half + y * rows + h * piece, piece)
         return remote(
-            parts.at[p, t, own], z_in.at[p, k, t], zp_s.at[p, k, t], zp_r.at[p, k, t], line(k)
+            parts.at[p, t, pl.ds(start, piece)],
+            z_in.at[p, k, t, pl.ds(h * piece, piece)],
+            zp_s.at[p, k, t, h],
+            zp_r.at[p, k, t, h],
+            line(k),
         )
 
     def x_out(p):
@@ -310,8 +317,8 @@
             ).astype(jnp.bfloat16)
 
     def along_line(p, t):
-        def total(received):
-            @pl.loop(0, rows // 16)
+        def total(received, h):
+            @pl.loop(h * piece // 16, (h + 1) * piece // 16)
             def _(n):
                 here = pl.ds(pl.multiple_of(half + y * rows + n * 16, 16), 16)
                 there = pl.ds(pl.multiple_of(n * 16, 16), 16)
@@ -325,19 +332,22 @@
 
             @pl.when(beyond & outermost)
             def _(k=k):
-                total(None)
-                z_parts(p, t, k).start()
+                for h in range(2):
+                    total(None, h)
+                    z_parts(p, t, k, h).start()
 
             @pl.when(beyond & jnp.logical_not(outermost))
             def _(k=k):
-                z_parts(p, t, k).wait_recv()
-                total(k)
-                z_parts(p, t, k).start()
+                for h in range(2):
+                    z_parts(p, t, k, h).wait_recv()
+                    total(k, h)
+                    z_parts(p, t, k, h).start()
 
     def complete(p, source):
         y_parts(p, z).wait_recv()
-        pl.when(z > 0)(lambda: z_parts(p, z, 0).wait_recv())
-        pl.when(z < nz - 1)(lambda: z_parts(p, z, 1).wait_recv())
+        for h in range(2):
+            pl.when(z > 0)(lambda h=h: z_parts(p, z, 0, h).wait_recv())
+            pl.when(z < nz - 1)(lambda h=h: z_parts(p, z, 1, h).wait_recv())
 
         def add(received):
             @pl.loop(0, rows // 16)
@@ -386,25 +396,31 @@
 
             finish(p, near_first(distance - 1, z, nz), lambda: None)
 
-        def own_plane(p=p):
-            both_cores(p, z)
-            y_parts(p, z).start()
+        nearest = near_first(1, z, nz)
+        outermost = (z == 0) | (z == nz - 1)
+
+        def nearest_plane(p=p):
+            both_cores(p, nearest)
+            y_parts(p, nearest).start()
 
         farthest = near_first(nz - 1, z, nz)
-        finish(p, farthest, own_plane)
+        finish(p, farthest, nearest_plane)
         both_cores(p, farthest)
         y_parts(p, farthest).start()
-
-        @pl.loop(1, nz)
+        y_parts(p, nearest).wait_recv()
+        pl.when(outermost)(lambda: along_line(p, nearest))
+
+        @pl.loop(1, nz - 1)
         def _(back, p=p):
             t = near_first(nz - back, z, nz)
-            following = near_first(nz - back - 1, z, nz)
-            more = back < nz - 1
-            pl.when(more)(lambda: both_cores(p, following))
+            order = nz - back - 1
+            following = near_first(jnp.where(order > 1, order, 0), z, nz)
+            both_cores(p, following)
             y_parts(p, t).wait_recv()
-            pl.when(more)(lambda: y_parts(p, following).start())
+            y_parts(p, following).start()
             along_line(p, t)
 
+        pl.when(jnp.logical_not(outermost))(lambda: along_line(p, nearest))
         complete(p, source)
         if p < micro - 1:
 
@@ -432,11 +448,13 @@
 
             @pl.when(t > z)
             def _():
-                z_parts(p, t, 0).wait_send()
+                for h in range(2):
+                    z_parts(p, t, 0, h).wait_send()
 
             @pl.when(t < z)
             def _():
-                z_parts(p, t, 1).wait_send()
+                for h in range(2):
+                    z_parts(p, t, 1, h).wait_send()
 
         if p < micro - 1:
 
@@ -477,7 +495,7 @@
         + [sem((micro, nz))] * 2
         + [sem((micro, nz, 2))] * 2
         + [sem((micro, nz))] * 4
-        + [sem((micro, 2, nz))] * 2
+        + [sem((micro, 2, nz, 2))] * 2
         + [sem((micro,))] * 2,
         compiler_params=pltpu.CompilerParams(
             collective_id=0, has_side_effects=True, vmem_limit_bytes=60 * 1024 * 1024
@@ -506,6 +524,6 @@
     positions = {getattr(device, "coords", (0, 0, 0))[1] for device in mesh.devices.flat}
     line = mesh.shape["expert"] // 2
     body = shards
-    if len(positions) == 2 and mesh.shape["dp"] == 2 and 2 <= line <= 4:
+    if len(positions) == 2 and mesh.shape["dp"] == 2 and 3 <= line <= 4:
         body = functools.partial(fused_shards, line)
     return jax.shard_map(body, mesh=mesh, in_specs=in_specs, out_specs=out_specs, check_vma=False)

time: 171 us -> 170 us (level); the launches traced: 171 us -> 168 us
  Pallas kernels: 167 us -> 164 us
    pallas_call x1, Pallas kernels: 167 us -> 164 us  [fused_shards(): pl.pallas_call(functools.partial(fused_kernel, nz, segments, experts), ou...]
where the time goes in v4:
time: 170 us; the launch traced here: 168 us
  Pallas kernels  164 us (96%)
  local copies, waits for them, and re-layouts  3.39 us (2%)
    pallas_call x1, Pallas kernels, fused_shards(): pl.pallas_call(functools.partial(fused_kernel, nz, segments, experts), ou...  164 us

profile of v4, /device:TPU:10, one launch (start us, length us, event | category | flops | bytes accessed | tf_op | source)
XLA Modules:
  0.0 167.5 jit_solution(1650184742067897047)
XLA Ops:
  0.0 1.4 copy.9
  1.4 164.1 %shard_map.82 = bf16[2,64,2560]{2,1,0:T(8,128)(2,1)} custom-call(bf16[64,2560]{1,0:T(8,128)(2,1)} %bitcast.8, bf16[1,64,2560]{2,1,0:T(8,128)(2,1)} %fresh_ref.1, s32[2,64,6]{2,1,0:T(8,128)} %bitcast.7, bf16[16,2560]{1,0:T(8,128)(2,1)} %bitcast.9, f32[1,2560]{1,0:T(1,128)} %gain_ref.1, bf16[1,1,2560,768]{3,2,1,0:T(8,128)(2,1)} %gate_hbm.1, ...), custom_call_target="tpu_custom_call" | custom-call | flops 24159191040 | bytes 11796480 | tf_op jit(solution)/shard_map/pallas_call | solution.py:475
  165.6 2.0 %copy.11 = bf16[1,2,64,2560]{3,2,1,0:T(8,128)(2,1)} copy(bf16[1,2,64,2560]{3,2,1,0:T(8,128)(2,1)} %bitcast.6) | data formatting | bytes 1310720
